TPU v7x, 32 devices: a whole 2x2x4 slice. The times are simulated.
32 devices in a mesh: src: 2 (over z_hi), lat: 8 (over y, x, core), sub: 2 (over z_lo).
Axes of the slice: x: 2, y: 2, z: 4 (z_hi: 2, z_lo: 2; z = z_hi * 2 + z_lo), core: 2. Of those that a mesh axis runs over, the one named last changes fastest.
Arguments:
- sources: float32 [2, 24, 96, 2, 128], P(None, None, ('lat', 'sub'), 'src'), may hold values from -6 to 6
- eigvecs: bfloat16 [32, 24, 96, 2, 128], P(None, None, ('lat', 'sub'), 'src'), may hold values from -6 to 6
- eigvals: float32 [32], replicated, may hold values from 0.5 to 8
- links: float32 [4, 18, 96, 2, 128], P(None, None, ('lat', 'sub')), may hold values from -6 to 6
- damping: float32 [2], P('src'), may hold values from 0.5 to 1
Outputs:
- guess: float32 [2, 24, 96, 2, 128], P(None, None, ('lat', 'sub'), 'src')
- solution: float32 [2, 24, 96, 2, 128], P(None, None, ('lat', 'sub'), 'src')
All inputs are finite; a program needn't handle non-finite values.
Results may differ from a plain program's by a relative error of at most 0.0047.
Values sent between devices are 32-bit elements; how exact they have to be, the bound alone decides.
A program may use at most 64 MiB of HBM per device.

v0:
```python
import math

import jax
import jax.numpy as jnp
import numpy as np
from jax import lax
from jax.sharding import PartitionSpec as P

LX = 16
ITERS = 2


HOPPING = 0.12
SPIN_BLOCKS = [
    (np.array([[0.0, 0.0], [0.0, 0.0]]), np.array([[0.0, 1.0], [1.0, 0.0]])),
    (np.array([[0.0, -1.0], [1.0, 0.0]]), np.zeros((2, 2))),
    (np.array([[0.0, 0.0], [0.0, 0.0]]), np.array([[1.0, 0.0], [0.0, -1.0]])),
    (np.eye(2), np.zeros((2, 2))),
]


def passed_along(x, axis, by):
    devices = lax.axis_size(axis)
    return lax.ppermute(x, axis, [(i, (i + by) % devices) for i in range(devices)])


def spin_apply(table_re, table_im, real_part, imag_part):
    rows_re = []
    rows_im = []
    for row in range(2):
        acc_re = (
            float(table_re[row, 0]) * real_part[:, 0] - float(table_im[row, 0]) * imag_part[:, 0]
        )
        acc_im = (
            float(table_re[row, 0]) * imag_part[:, 0] + float(table_im[row, 0]) * real_part[:, 0]
        )
        acc_re = (
            acc_re
            + float(table_re[row, 1]) * real_part[:, 1]
            - float(table_im[row, 1]) * imag_part[:, 1]
        )
        acc_im = (
            acc_im
            + float(table_re[row, 1]) * imag_part[:, 1]
            + float(table_im[row, 1]) * real_part[:, 1]
        )
        rows_re.append(acc_re)
        rows_im.append(acc_im)
    return (jnp.stack(rows_re, 1), jnp.stack(rows_im, 1))


def project(sign, direction, real_part, imag_part):
    table_re, table_im = SPIN_BLOCKS[direction]
    lower_re, lower_im = spin_apply(table_re, table_im, real_part[:, 2:], imag_part[:, 2:])
    return (real_part[:, :2] + sign * lower_re, imag_part[:, :2] + sign * lower_im)


def rebuild(sign, direction, upper_re, upper_im):
    table_re, table_im = SPIN_BLOCKS[direction]
    lower_re, lower_im = spin_apply(table_re.T, -table_im.T, upper_re, upper_im)
    return (
        jnp.concatenate([upper_re, sign * lower_re], 1),
        jnp.concatenate([upper_im, sign * lower_im], 1),
    )


def color_mul(links_re, links_im, real_part, imag_part):
    rows_re = []
    rows_im = []
    for row in range(3):
        acc_re = links_re[row, 0] * real_part[:, :, 0] - links_im[row, 0] * imag_part[:, :, 0]
        acc_im = links_re[row, 0] * imag_part[:, :, 0] + links_im[row, 0] * real_part[:, :, 0]
        for col in range(1, 3):
            acc_re = (
                acc_re
                + links_re[row, col] * real_part[:, :, col]
                - links_im[row, col] * imag_part[:, :, col]
            )
            acc_im = (
                acc_im
                + links_re[row, col] * imag_part[:, :, col]
                + links_im[row, col] * real_part[:, :, col]
            )
        rows_re.append(acc_re)
        rows_im.append(acc_im)
    return (jnp.stack(rows_re, 2), jnp.stack(rows_im, 2))


def color_adj(links_re, links_im, real_part, imag_part):
    rows_re = []
    rows_im = []
    for row in range(3):
        acc_re = links_re[0, row] * real_part[:, :, 0] + links_im[0, row] * imag_part[:, :, 0]
        acc_im = links_re[0, row] * imag_part[:, :, 0] - links_im[0, row] * real_part[:, :, 0]
        for col in range(1, 3):
            acc_re = (
                acc_re
                + links_re[col, row] * real_part[:, :, col]
                + links_im[col, row] * imag_part[:, :, col]
            )
            acc_im = (
                acc_im
                + links_re[col, row] * imag_part[:, :, col]
                - links_im[col, row] * real_part[:, :, col]
            )
        rows_re.append(acc_re)
        rows_im.append(acc_im)
    return (jnp.stack(rows_re, 2), jnp.stack(rows_im, 2))


def link_parts(links, direction):
    extent = links.shape[2:]
    return (
        links[direction, :9].reshape((3, 3) + extent),
        links[direction, 9:].reshape((3, 3) + extent),
    )


def neighbour(values, direction, step):
    if direction == 0:
        column = jnp.arange(values.shape[-1]) % LX
        border = LX - 1 if step > 0 else 0
        inside = jnp.roll(values, -step, axis=-1)
        wrapped = jnp.roll(values, step * (LX - 1), axis=-1)
        return jnp.where(column == border, wrapped, inside)
    if direction == 1:
        return jnp.roll(values, -step * LX, axis=-1)
    return jnp.roll(values, -step, axis=-2)


def split_parts(spinor):
    count = spinor.shape[0]
    extent = spinor.shape[2:]
    return (
        spinor[:, :12].reshape((count, 4, 3) + extent),
        spinor[:, 12:].reshape((count, 4, 3) + extent),
    )


def join_parts(real_part, imag_part):
    count = real_part.shape[0]
    extent = real_part.shape[3:]
    return jnp.concatenate(
        [real_part.reshape((count, 12) + extent), imag_part.reshape((count, 12) + extent)], 1
    )


def shards(sources, eigvecs, eigvals, links, damping):
    count = sources.shape[0]
    flat_src = sources.astype(jnp.bfloat16).reshape(count, 24, -1)
    swapped = jnp.concatenate([flat_src[:, 12:], -flat_src[:, :12]], 1)
    stacked = jnp.concatenate([flat_src, swapped], 0).reshape(2 * count, -1)
    flat_vec = eigvecs.reshape(eigvecs.shape[0], -1)
    partial_value = lax.dot_general(
        flat_vec, stacked, (((1,), (1,)), ((), ())), preferred_element_type=jnp.float32
    )
    correlation = lax.psum(partial_value, ("src", "lat", "sub"))
    sites_all = flat_vec.shape[1] // 24 * lax.axis_size(("src", "lat", "sub"))
    correlation = correlation / math.sqrt(24 * sites_all)
    weights = (
        jnp.concatenate([correlation[:, :count].T, correlation[:, count:].T], 0) / eigvals[None, :]
    )
    weights = weights.astype(jnp.bfloat16)
    mixed = jnp.dot(weights, flat_vec, preferred_element_type=jnp.float32)
    middle = mixed.shape[1] // 2
    guess = jnp.concatenate(
        [
            mixed[:count, :middle] - mixed[count:, middle:],
            mixed[:count, middle:] + mixed[count:, :middle],
        ],
        1,
    ).reshape(sources.shape)
    source, iterate = (
        lax.all_to_all(sources, "src", split_axis=0, concat_axis=3, tiled=True),
        lax.all_to_all(guess, "src", split_axis=0, concat_axis=3, tiled=True),
    )
    extent = lax.axis_size(("lat", "sub"))
    place = lax.axis_index(("lat", "sub"))
    slices = links.shape[2]
    slice_index = jnp.arange(slices)
    top_flip = jnp.where(place == extent - 1, -1.0, 1.0)
    bottom_flip = jnp.where(place == 0, -1.0, 1.0)
    top_sign = jnp.where(slice_index == slices - 1, top_flip, 1.0).astype(jnp.float32)[
        :, None, None
    ]
    bottom_sign = jnp.where(slice_index == 0, bottom_flip, 1.0).astype(jnp.float32)[:, None, None]
    time_re, time_im = link_parts(links, 3)
    space_links = []
    for direction in range(3):
        links_re, links_im = link_parts(links, direction)
        space_links.append(
            (
                links_re,
                links_im,
                neighbour(links_re, direction, -1),
                neighbour(links_im, direction, -1),
            )
        )
    rate = damping[:, None, None, None, None]
    for sweep in range(ITERS):
        real_part, imag_part = split_parts(iterate)
        terms = []
        for apply_direction in range(3):
            apply_links_re, apply_links_im, behind_lre, behind_lim = space_links[apply_direction]
            ahead_re = neighbour(real_part, apply_direction, 1)
            ahead_im = neighbour(imag_part, apply_direction, 1)
            carried = color_mul(apply_links_re, apply_links_im, ahead_re, ahead_im)
            terms.append(rebuild(-1.0, apply_direction, *project(-1.0, apply_direction, *carried)))
            behind_re = neighbour(real_part, apply_direction, -1)
            behind_im = neighbour(imag_part, apply_direction, -1)
            carried = color_adj(behind_lre, behind_lim, behind_re, behind_im)
            terms.append(rebuild(1.0, apply_direction, *project(1.0, apply_direction, *carried)))
        upper_re, upper_im = project(-1.0, 3, real_part, imag_part)
        sent_up = jnp.stack([upper_re[:, :, :, :1], upper_im[:, :, :, :1]], 1)
        got_up = passed_along(sent_up, ("lat", "sub"), -1)
        ahead_re = jnp.concatenate([upper_re[:, :, :, 1:], got_up[:, 0]], 3) * top_sign
        ahead_im = jnp.concatenate([upper_im[:, :, :, 1:], got_up[:, 1]], 3) * top_sign
        terms.append(rebuild(-1.0, 3, *color_mul(time_re, time_im, ahead_re, ahead_im)))
        lower_re, lower_im = project(1.0, 3, *color_adj(time_re, time_im, real_part, imag_part))
        sent_down = jnp.stack([lower_re[:, :, :, slices - 1 :], lower_im[:, :, :, slices - 1 :]], 1)
        got_down = passed_along(sent_down, ("lat", "sub"), 1)
        behind_re = (
            jnp.concatenate([got_down[:, 0], lower_re[:, :, :, : slices - 1]], 3) * bottom_sign
        )
        behind_im = (
            jnp.concatenate([got_down[:, 1], lower_im[:, :, :, : slices - 1]], 3) * bottom_sign
        )
        terms.append(rebuild(1.0, 3, behind_re, behind_im))
        total_re, total_im = terms[0]
        for extra in terms[1:]:
            total_re = total_re + extra[0]
            total_im = total_im + extra[1]
        iterate = iterate + rate * (source - (iterate - HOPPING * join_parts(total_re, total_im)))
    solution = lax.all_to_all(iterate, "src", split_axis=3, concat_axis=0, tiled=True)
    return (guess, solution)


def solution(mesh):
    return jax.shard_map(
        shards,
        mesh=mesh,
        in_specs=(
            P(None, None, ("lat", "sub"), "src", None),
            P(None, None, ("lat", "sub"), "src", None),
            P(),
            P(None, None, ("lat", "sub"), None, None),
            P("src"),
        ),
        out_specs=(
            P(None, None, ("lat", "sub"), "src", None),
            P(None, None, ("lat", "sub"), "src", None),
        ),
        check_vma=False,
    )
```

profile of v0, /device:TPU:0, one launch (start us, length us, event | category | flops | bytes accessed | tf_op | source)
XLA Modules:
  0.0 96.5 jit_solution(1236982175737722736)
XLA Ops:
  0.6 1.3 %convert_reduce_fusion = bf16[2,24,6,128]{3,2,1,0:T(8,128)(2,1)S(1)} fusion(f32[2,24,6,1,128]{4,3,2,1,0:T(1,128)} %param.5), kind=kLoop, calls=%fused_computation.17 | loop fusion | flops 36864 | bytes 221184 | tf_op jit(solution)/shard_map/convert_element_type | solution.py:150
  2.2 1.7 %copy.303 = bf16[32,24,6,1,128]{4,2,1,0,3:T(8,128)(2,1)S(1)} copy(bf16[32,24,6,1,128]{4,1,3,2,0:T(8,128)(2,1)} %param.6) | data formatting | bytes 2359296 | tf_op args[1]
  3.9 1.3 %reshape.6262 = bf16[32,18432]{1,0:T(8,128)(2,1)S(1)} reshape(bf16[32,24,6,1,128]{4,2,1,0,3:T(8,128)(2,1)S(1)} %copy.303) | data formatting | bytes 2359296 | tf_op jit(solution)/shard_map/reshape | solution.py:153
  5.2 0.4 convolution_bitcast_fusion
  5.6 42.0 %psum.7 = f32[32,4]{0,1:T(4,128)S(1)} all-reduce(f32[32,4]{0,1:T(4,128)S(1)} %convolution_bitcast_fusion), channel_id=1, replica_groups=mesh['src'=2,'lat'=8,'sub'=2] {'src','lat','sub'}, use_global_device_ids=true, to_apply=%region_0.0 | all-reduce | flops 128 | bytes 1024 | tf_op jit(solution)/shard_map/psum | solution.py:157
  47.6 0.3 fusion.107
  48.2 0.7 copy.304
  48.9 3.6 %all-to-all-start = ((f32[2,24,6,1,128]{4,1,3,2,0:T(8,128)}), f32[2,24,6,1,128]{4,1,3,2,0:T(8,128)S(1)}, u32[]{:S(2)}, u32[]{:S(2)}) async-start(f32[2,24,6,1,128]{4,1,3,2,0:T(8,128)} %copy.304), calls=%async_computation | async-start | bytes 294912 | tf_op jit(solution)/shard_map/all_to_all | solution.py:175
  53.9 0.3 maximum_select_fusion.8
  54.3 0.7 copy.305
  55.7 2.3 %all-to-all-done = f32[2,24,6,1,128]{4,1,3,2,0:T(8,128)S(1)} async-done(((f32[2,24,6,1,128]{4,1,3,2,0:T(8,128)}), f32[2,24,6,1,128]{4,1,3,2,0:T(8,128)S(1)}, u32[]{:S(2)}, u32[]{:S(2)}) %all-to-all-start) | async-done | bytes 147488 | tf_op jit(solution)/shard_map/all_to_all | solution.py:175
  58.0 3.4 %all-to-all-start.1 = ((f32[2,24,6,1,128]{4,1,3,2,0:T(8,128)}), f32[2,24,6,1,128]{4,1,3,2,0:T(8,128)S(1)}, u32[]{:S(2)}, u32[]{:S(2)}) async-start(f32[2,24,6,1,128]{4,1,3,2,0:T(8,128)} %copy.305), calls=%async_computation.1 | async-start | bytes 294912 | tf_op jit(solution)/shard_map/all_to_all | solution.py:174
  61.5 0.1 fusion.153
  61.6 0.1 fusion.154
  61.8 0.1 fusion.155
  61.9 0.1 fusion.156
  62.1 0.1 fusion.157
  62.3 0.1 fusion.158
  62.4 0.1 fusion.159
  62.6 0.1 fusion.160
  62.7 0.2 fusion.162
  63.0 0.2 fusion.161
  63.5 0.6 collective-permute-start
  64.5 1.8 %collective-permute-start.1 = (f32[1,2,2,3,1,2,128]{6,5,3,2,4,1,0:T(2,128)S(1)}, f32[1,2,2,3,1,2,128]{6,5,3,2,4,1,0:T(2,128)S(1)}, u32[]{:S(2)}, u32[]{:S(2)}) collective-permute-start(f32[1,2,2,3,1,2,128]{6,5,3,2,4,1,0:T(2,128)S(1)} %pad_maximum_fusion.118), channel_id=1, source_target_pairs={{0,1},{1,2},{2,3},{3,4},{4,5},{5,6},{6,7},{7,8},{8,9},{9,10},{10,1... | collective-permute-start | bytes 36872 | tf_op jit(solution)/shard_map/ppermute | solution.py:24
  66.3 0.7 maximum_select_fusion
  67.5 0.2 multiply_subtract_fusion.35
  67.8 0.1 multiply_subtract_fusion.34
  68.3 0.2 multiply_subtract_fusion.29
  68.5 0.2 multiply_subtract_fusion.27
  68.6 0.2 multiply_subtract_fusion.28
  68.8 0.1 multiply_add_fusion.26
  69.8 0.2 multiply_add_fusion.32
  70.0 0.1 multiply_add_fusion.31
  71.6 0.2 maximum_add_fusion.1
  71.8 0.2 maximum_add_fusion.3
  72.2 0.1 fusion.139
  72.3 0.1 fusion.140
  72.5 0.1 fusion.141
  72.6 0.1 fusion.142
  72.9 0.1 fusion.143
  73.0 0.1 fusion.144
  73.2 0.1 fusion.145
  73.3 0.1 fusion.146
  73.5 0.4 maximum_select_fusion.4
  74.1 0.1 fusion.147
  74.3 0.1 fusion.148
  74.4 0.1 fusion.149
  74.6 0.1 fusion.150
  74.7 0.2 multiply_subtract_fusion.14
  75.3 0.2 multiply_subtract_fusion.8
  75.5 0.2 multiply_subtract_fusion.6
  75.6 0.2 multiply_subtract_fusion.7
  76.0 0.4 maximum_select_fusion.6
  76.6 0.2 multiply_add_fusion.11
  77.4 2.1 %collective-permute-start.2 = (f32[1,2,2,3,1,2,128]{6,5,3,2,4,1,0:T(2,128)S(1)}, f32[1,2,2,3,1,2,128]{6,5,3,2,4,1,0:T(2,128)S(1)}, u32[]{:S(2)}, u32[]{:S(2)}) collective-permute-start(f32[1,2,2,3,1,2,128]{6,5,3,2,4,1,0:T(2,128)S(1)} %pad_maximum_fusion.119), channel_id=1, source_target_pairs={{0,15},{1,0},{2,1},{3,2},{4,3},{5,4},{6,5},{7,6},{8,7},{9,8},{10,9... | collective-permute-start | bytes 36872 | tf_op jit(solution)/shard_map/ppermute | solution.py:24
  79.7 0.3 collective-permute-start.3
  82.4 2.5 %collective-permute-done.3 = f32[1,2,2,3,1,2,128]{6,5,3,2,4,1,0:T(2,128)S(1)} collective-permute-done((f32[1,2,2,3,1,2,128]{6,5,3,2,4,1,0:T(2,128)S(1)}, f32[1,2,2,3,1,2,128]{6,5,3,2,4,1,0:T(2,128)S(1)}, u32[]{:S(2)}, u32[]{:S(2)}) %collective-permute-start.3) | collective-permute-done | bytes 12320 | tf_op jit(solution)/shard_map/ppermute | solution.py:24
  85.1 0.2 maximum_add_fusion.5
  85.3 0.2 maximum_add_fusion.7
  85.5 0.7 fusion.11
  86.3 3.9 %all-to-all-start.2 = ((f32[1,24,6,2,128]{4,1,2,0,3:T(8,128)}), f32[1,24,6,2,128]{4,1,2,0,3:T(8,128)S(1)}, u32[]{:S(2)}, u32[]{:S(2)}) async-start(f32[1,24,6,2,128]{4,1,2,0,3:T(8,128)} %fusion.11), calls=%async_computation.2 | async-start | bytes 294912 | tf_op jit(solution)/shard_map/all_to_all | solution.py:234
  90.2 0.8 copy.316
  91.0 4.7 %all-to-all-done.2 = f32[1,24,6,2,128]{4,1,2,0,3:T(8,128)S(1)} async-done(((f32[1,24,6,2,128]{4,1,2,0,3:T(8,128)}), f32[1,24,6,2,128]{4,1,2,0,3:T(8,128)S(1)}, u32[]{:S(2)}, u32[]{:S(2)}) %all-to-all-start.2) | async-done | bytes 147488 | tf_op jit(solution)/shard_map/all_to_all | solution.py:234
  95.7 0.8 copy.317
  (226 shorter events, 9.6 us)
Async XLA Ops:
  5.2 42.4 %copy-start.2 = (f32[32]{0:T(128)S(1)}, f32[32]{0:T(128)}, u32[]{:S(2)}) copy-start(f32[32]{0:T(128)} %param.7) | copy-start | bytes 388
  47.9 4.6 %copy-start.1 = (f32[4,18,6,2,128]{4,3,2,1,0:T(2,128)S(1)}, f32[4,18,6,2,128]{4,3,2,1,0:T(2,128)}, u32[]{:S(2)}) copy-start(f32[4,18,6,2,128]{4,3,2,1,0:T(2,128)} %param.8) | copy-start | bytes 1327108
  48.9 9.1 %all-to-all-start = ((f32[2,24,6,1,128]{4,1,3,2,0:T(8,128)}), f32[2,24,6,1,128]{4,1,3,2,0:T(8,128)S(1)}, u32[]{:S(2)}, u32[]{:S(2)}) async-start(f32[2,24,6,1,128]{4,1,3,2,0:T(8,128)} %copy.304), calls=%async_computation | async-start | bytes 294912 | tf_op jit(solution)/shard_map/all_to_all | solution.py:175
  53.0 1.3 %copy-start = (f32[2,24,6,1,128]{4,3,2,1,0:T(1,128)S(1)}, f32[2,24,6,1,128]{4,3,2,1,0:T(1,128)}, u32[]{:S(2)}) copy-start(f32[2,24,6,1,128]{4,3,2,1,0:T(1,128)} %param.5) | copy-start | bytes 442372
  58.0 14.1 %all-to-all-start.1 = ((f32[2,24,6,1,128]{4,1,3,2,0:T(8,128)}), f32[2,24,6,1,128]{4,1,3,2,0:T(8,128)S(1)}, u32[]{:S(2)}, u32[]{:S(2)}) async-start(f32[2,24,6,1,128]{4,1,3,2,0:T(8,128)} %copy.305), calls=%async_computation.1 | async-start | bytes 294912 | tf_op jit(solution)/shard_map/all_to_all | solution.py:174
  63.5 7.5 %collective-permute-start = (f32[1,2,2,3,1,2,128]{6,5,3,2,4,1,0:T(2,128)S(1)}, f32[1,2,2,3,1,2,128]{6,5,3,2,4,1,0:T(2,128)S(1)}, u32[]{:S(2)}, u32[]{:S(2)}) collective-permute-start(f32[1,2,2,3,1,2,128]{6,5,3,2,4,1,0:T(2,128)S(1)} %pad_maximum_fusion.117), channel_id=1, source_target_pairs={{0,15},{1,0},{2,1},{3,2},{4,3},{5,4},{6,5},{7,6},{8,7},{9,8},{10,9... | collective-permute-start | bytes 36872 | tf_op jit(solution)/shard_map/ppermute | solution.py:24
  64.5 6.9 %collective-permute-start.1 = (f32[1,2,2,3,1,2,128]{6,5,3,2,4,1,0:T(2,128)S(1)}, f32[1,2,2,3,1,2,128]{6,5,3,2,4,1,0:T(2,128)S(1)}, u32[]{:S(2)}, u32[]{:S(2)}) collective-permute-start(f32[1,2,2,3,1,2,128]{6,5,3,2,4,1,0:T(2,128)S(1)} %pad_maximum_fusion.118), channel_id=1, source_target_pairs={{0,1},{1,2},{2,3},{3,4},{4,5},{5,6},{6,7},{7,8},{8,9},{9,10},{10,1... | collective-permute-start | bytes 36872 | tf_op jit(solution)/shard_map/ppermute | solution.py:24
  77.4 4.6 %collective-permute-start.2 = (f32[1,2,2,3,1,2,128]{6,5,3,2,4,1,0:T(2,128)S(1)}, f32[1,2,2,3,1,2,128]{6,5,3,2,4,1,0:T(2,128)S(1)}, u32[]{:S(2)}, u32[]{:S(2)}) collective-permute-start(f32[1,2,2,3,1,2,128]{6,5,3,2,4,1,0:T(2,128)S(1)} %pad_maximum_fusion.119), channel_id=1, source_target_pairs={{0,15},{1,0},{2,1},{3,2},{4,3},{5,4},{6,5},{7,6},{8,7},{9,8},{10,9... | collective-permute-start | bytes 36872 | tf_op jit(solution)/shard_map/ppermute | solution.py:24
  79.7 5.2 %collective-permute-start.3 = (f32[1,2,2,3,1,2,128]{6,5,3,2,4,1,0:T(2,128)S(1)}, f32[1,2,2,3,1,2,128]{6,5,3,2,4,1,0:T(2,128)S(1)}, u32[]{:S(2)}, u32[]{:S(2)}) collective-permute-start(f32[1,2,2,3,1,2,128]{6,5,3,2,4,1,0:T(2,128)S(1)} %pad_maximum_fusion.120), channel_id=1, source_target_pairs={{0,1},{1,2},{2,3},{3,4},{4,5},{5,6},{6,7},{7,8},{8,9},{9,10},{10,1... | collective-permute-start | bytes 36872 | tf_op jit(solution)/shard_map/ppermute | solution.py:24
  86.3 9.4 %all-to-all-start.2 = ((f32[1,24,6,2,128]{4,1,2,0,3:T(8,128)}), f32[1,24,6,2,128]{4,1,2,0,3:T(8,128)S(1)}, u32[]{:S(2)}, u32[]{:S(2)}) async-start(f32[1,24,6,2,128]{4,1,2,0,3:T(8,128)} %fusion.11), calls=%async_computation.2 | async-start | bytes 294912 | tf_op jit(solution)/shard_map/all_to_all | solution.py:234
where the time goes:
time: 96.9 us; the launch traced here: 96.5 us
  blocking collectives  42 us (43%)
  starting transfers between devices  15.6 us (16%)
  other arithmetic  14.4 us (15%)
  local copies, waits for them, and re-layouts  11.3 us (12%)
  waiting for transfers between devices  9.44 us (10%)
  between operations  3.03 us (3%)
    psum x1, blocking collectives, shards(): correlation = lax.psum(partial_value, ('src', 'lat', 'sub'))  42 us
    ppermute x4, starting transfers between devices, passed_along(): lax.ppermute(x, axis, [(i, (i + by) % devices) for i in range(devices)])  4.7 us
    all_to_all x1, waiting for transfers between devices, shards(): lax.all_to_all(iterate, 'src', split_axis=3, concat_axis=0, tiled=True)  4.67 us
    unnamed x11, local copies, waits for them, and re-layouts  4.03 us
    all_to_all x1, starting transfers between devices, shards(): lax.all_to_all(iterate, 'src', split_axis=3, concat_axis=0, tiled=True)  3.89 us
    all_to_all x1, starting transfers between devices, shards(): lax.all_to_all(guess, 'src', split_axis=0, concat_axis=3, tiled=True)  3.59 us
    all_to_all x1, starting transfers between devices, shards(): lax.all_to_all(sources, 'src', split_axis=0, concat_axis=3, tiled=True)  3.42 us
    sub x24, other arithmetic, color_mul(): acc_re + links_re[row, col] * real_part[:, :, col]  2.62 us
  transfers between devices with their start and end apart: 7, of which 3 were waited for; matrix products, arithmetic and copies ran while one was open for 13% of the time, Pallas kernels for 0%

commit v1 on v0

v1 whole, which is shorter than its diff:
```python
import functools
import math

import jax
import jax.numpy as jnp
from jax import lax
from jax.experimental import pallas as pl
from jax.experimental.pallas import tpu as pltpu
from jax.sharding import PartitionSpec as P

LX = 16
HOPPING = 0.12
MESH = pl.DeviceIdType.MESH

BLOCKS = [((1, 1), (0, 1)), ((1, 2), (0, 0)), ((0, 1), (1, 3)), ((0, 0), (1, 0))]
BLOCKS_H = [((1, 3), (0, 3)), ((1, 0), (0, 2)), ((0, 3), (1, 1)), ((0, 0), (1, 0))]


def add_phase(a, b, power):
    power %= 4
    if power == 0:
        return a[0] + b[0], a[1] + b[1]
    if power == 1:
        return a[0] - b[1], a[1] + b[0]
    if power == 2:
        return a[0] - b[0], a[1] - b[1]
    return a[0] + b[1], a[1] - b[0]


def project(sign, d, x):
    turn = 0 if sign > 0 else 2
    return [add_phase(x[r], x[2 + BLOCKS[d][r][0]], BLOCKS[d][r][1] + turn) for r in range(2)]


def rebuild(sign, d, half, acc):
    turn = 0 if sign > 0 else 2
    out = [add_phase(acc[r], half[r], 0) for r in range(2)]
    for r in range(2):
        col, power = BLOCKS_H[d][r]
        out.append(add_phase(acc[2 + r], half[col], power + turn))
    return out


def color_mul(u, half):
    ur, ui = u
    out = []
    for hr, hi in half:
        re = im = None
        for c in range(3):
            a, b = ur[:, c], ui[:, c]
            x, y = hr[c][None], hi[c][None]
            tr, ti = a * x - b * y, a * y + b * x
            re, im = (tr, ti) if re is None else (re + tr, im + ti)
        out.append((re, im))
    return out


def color_adj(u, half):
    ur, ui = u
    out = []
    for hr, hi in half:
        re = im = None
        for c in range(3):
            a, b = ur[c], ui[c]
            x, y = hr[c][None], hi[c][None]
            tr, ti = a * x + b * y, a * y - b * x
            re, im = (tr, ti) if re is None else (re + tr, im + ti)
        out.append((re, im))
    return out


def each(half, fn):
    return [(fn(re), fn(im)) for re, im in half]


def distinct(offsets, n):
    out = []
    for o in offsets:
        if o % n not in out:
            out.append(o % n)
    return out


def kernel(
    shape, sizes,
    src, eig, eigvals, links, damping, guess, sol,
    sa, sb, corr, slots, w2, xe0, xe1, sr, le, hs, gs, hr0, gr0, hr1, gr1, acc_ref,
    ar_send, ar_recv, sr_send, sr_recv, xe_send, xe_recv, h_send, h_recv, g_send, g_recv,
    h1_sem, g1_sem,
):
    T, LZ, S, K, TP = shape
    n, L, U = sizes
    N = n * L * U
    NT = L * U
    V = T * 24
    d0 = distinct((0, 1, -1, 2, -2), n)
    d1 = distinct((0, 1, -1), n)
    dl = distinct((0, 1, -1, -2), n)
    rows = 2 * S * K // 128
    me_s, me_l, me_u = lax.axis_index("src"), lax.axis_index("lat"), lax.axis_index("sub")
    place = me_l * U + me_u
    me = me_s * NT + place

    def device(s_index, t_index):
        return {"src": s_index, "lat": lax.div(t_index, U), "sub": lax.rem(t_index, U)}

    def of(g):
        return device(lax.div(g, NT), lax.rem(g, NT))

    above, below = lax.rem(place + 1, NT), lax.rem(place + NT - 1, NT)
    top_flip = jnp.where(place == NT - 1, -1.0, 1.0).astype(jnp.float32)
    bottom_flip = jnp.where(place == 0, -1.0, 1.0).astype(jnp.float32)

    barrier = pltpu.get_barrier_semaphore()

    def greet(i, carry):
        pl.semaphore_signal(barrier, inc=1, device_id=of(lax.rem(me + i, N)), device_id_type=MESH)
        return carry

    lax.fori_loop(1, N, greet, 0)

    for s in range(S):
        for t in range(T):
            low = [
                src[pl.ds(s * V + p * 12 * T + t, 12, stride=T), :]
                .astype(jnp.bfloat16)
                .astype(jnp.float32)
                for p in range(2)
            ]
            sa[s, pl.ds(t * 24, 12), :] = low[0]
            sa[s, pl.ds(t * 24 + 12, 12), :] = low[1]
            sb[s, pl.ds(t * 24, 12), :] = low[1]
            sb[s, pl.ds(t * 24 + 12, 12), :] = -low[0]

    def correlate(k, carry):
        e = eig[k].astype(jnp.float32)
        for p, ref in enumerate((sa, sb)):
            for s in range(S):
                part = jnp.sum((e * ref[s]).reshape(V // 8, 8, 128), axis=0)
                corr[pl.ds((p * S + s) * K + k, 1), :] = jnp.sum(part, axis=0, keepdims=True)
        return carry

    lax.fori_loop(0, K, correlate, 0)
    flat = lax.dot_general(
        jnp.ones((8, 128), jnp.float32), corr[...], (((1,), (1,)), ((), ())),
        preferred_element_type=jnp.float32, precision=lax.Precision.HIGHEST,
    )
    for r in range(rows):
        slots[me, pl.ds(r, 1), :] = flat[0:1, r * 128 : (r + 1) * 128]
    slots[me, pl.ds(rows, 1), :] = jnp.full((1, 128), damping[0], jnp.float32)
    sr[0, pl.ds(0, S * V), :] = src[...]

    pl.semaphore_wait(barrier, N - 1)

    def spread(i, carry):
        pltpu.make_async_remote_copy(
            src_ref=slots.at[me], dst_ref=slots.at[me], send_sem=ar_send, recv_sem=ar_recv,
            device_id=of(lax.rem(me + i, N)), device_id_type=MESH,
        ).start()
        return carry

    lax.fori_loop(1, N, spread, 0)

    sent = []
    src_copies = {}
    for i, o in enumerate(d1):
        if o:
            copy = pltpu.make_async_remote_copy(
                src_ref=src, dst_ref=sr.at[i, pl.ds(0, S * V)],
                send_sem=sr_send.at[i], recv_sem=sr_recv.at[i],
                device_id=device(lax.rem(me_s + n - o, n), place), device_id_type=MESH,
            )
            copy.start()
            sent.append(copy)
            src_copies[i] = copy

    for i, o in enumerate(dl):
        z = lax.rem(me_s + o, n)

        def arrange(c, carry):
            le[i, c, pl.ds(0, T), :] = links[pl.ds(c * T * LZ + z, T, stride=LZ), :]
            return carry

        lax.fori_loop(0, 72, arrange, 0)

    every = slots.at[pl.ds(0, N - 1)]
    pltpu.make_async_copy(every, every, ar_recv).wait()
    total = jnp.sum(slots[...], axis=0)
    eye = lax.broadcasted_iota(jnp.int32, (128, 128), 0) == lax.broadcasted_iota(
        jnp.int32, (128, 128), 1
    )
    values = jnp.concatenate([eigvals[...]] * (128 // K), axis=1)
    scale = math.sqrt(24 * T * NT * LZ * 128)
    for r in range(rows):
        w = (total[r : r + 1] / scale / values).astype(jnp.bfloat16).astype(jnp.float32)
        w2[pl.ds(r * 128, 128), :] = jnp.dot(
            jnp.where(eye, w, 0.0).astype(jnp.bfloat16), jnp.ones((128, 128), jnp.bfloat16),
            preferred_element_type=jnp.float32,
        )

    def tile(ref, index):
        parts = [
            [
                jnp.stack([ref[index, pl.ds(p * 12 + sp * 3 + c, TP, stride=24), :] for c in range(3)])
                for sp in range(4)
            ]
            for p in range(2)
        ]
        return [(parts[0][sp], parts[1][sp]) for sp in range(4)]

    def link(o, d):
        i = dl.index(o % n)
        return (
            le[i, pl.ds(d * 18, 9)].reshape(3, 3, TP, 128),
            le[i, pl.ds(d * 18 + 9, 9)].reshape(3, 3, TP, 128),
        )

    def put_halo(buf, s, half, row):
        for p in range(2):
            for sp in range(2):
                buf[s, pl.ds(p * 6 + sp * 3, 3)] = half[sp][p][:, row : row + 1, :]

    def get_halo(buf, index, flip):
        return [
            tuple(buf[index, pl.ds(p * 6 + sp * 3, 3)] * flip for p in range(2)) for sp in range(2)
        ]

    def edges_all(ref, j):
        def body(s, carry):
            x = tile(ref, s)
            put_halo(hs.at[j], s, project(-1, 3, x), 0)
            put_halo(gs.at[j], s, color_adj(link(0, 3), project(1, 3, x)), T - 1)
            return carry

        lax.fori_loop(0, S, body, 0)

    def send_halo(buf, dest, send, recv, t_index, offsets):
        out = []
        for i, o in enumerate(offsets):
            copy = pltpu.make_async_remote_copy(
                src_ref=buf, dst_ref=dest.at[pl.ds(i * S, S)], send_sem=send.at[i],
                recv_sem=recv.at[i], device_id=device(lax.rem(me_s + n - o, n), t_index),
                device_id_type=MESH,
            )
            copy.start()
            out.append(copy)
        return out

    step = 48 if T % 2 == 0 else V
    chunks = list(range(V // step))
    order = [chunks[0]] + chunks[-1:0:-1]
    xe_copies = []
    h_copies = g_copies = None
    for done, ch in enumerate(order):

        def mix(k, acc):
            e = eig[k, pl.ds(ch * step, step), :].astype(jnp.float32)
            return tuple(
                a + w2[pl.ds(j * K + k, 1), :] * e for j, a in enumerate(acc)
            )

        acc = lax.fori_loop(
            0, K, mix, tuple(jnp.zeros((step, 128), jnp.float32) for _ in range(2 * S)), unroll=4
        )
        for s in range(S):
            one, two = acc[s], acc[S + s]
            for t in range(step // 24):
                b = t * 24
                turned = jnp.concatenate([-two[b + 12 : b + 24], two[b : b + 12]], axis=0)
                xe0[s, pl.ds(ch * step + b, 24), :] = one[b : b + 24] + turned
        if done == min(1, len(order) - 1):
            edges_all(xe0, 0)
            h_copies = send_halo(hs.at[0], hr0, h_send, h_recv, below, d1)
            g_copies = send_halo(gs.at[0], gr0, g_send, g_recv, above, d1)
        for i, o in enumerate(d0):
            if o:
                part = pl.ds(ch * step, step)
                copy = pltpu.make_async_remote_copy(
                    src_ref=xe0.at[pl.ds(0, S), part], dst_ref=xe0.at[pl.ds(i * S, S), part],
                    send_sem=xe_send.at[i, ch], recv_sem=xe_recv.at[i, ch],
                    device_id=device(lax.rem(me_s + n - o, n), place), device_id_type=MESH,
                )
                copy.start()
                xe_copies.append(copy)
    for s in range(S):
        for c in range(24):
            guess[pl.ds((s * 24 + c) * T, T), :] = xe0[s, pl.ds(c, T, stride=24), :]

    row = lax.broadcasted_iota(jnp.int32, (1, TP, 128), 1)
    column = lax.rem(lax.broadcasted_iota(jnp.int32, (1, TP, 128), 2), LX)

    def shift(v, d, by):
        if d == 0:
            border = LX - 1 if by > 0 else 0
            inside = pltpu.roll(v, (-by) % 128, 2)
            wrapped = pltpu.roll(v, (by * (LX - 1)) % 128, 2)
            return jnp.where(column == border, wrapped, inside)
        return pltpu.roll(v, (-by * LX) % 128, 2)

    def plane_hops(x, o, acc):
        for d in range(2):
            u = link(o, d)
            ahead = each(project(-1, d, x), lambda v: shift(v, d, 1))
            acc = rebuild(-1, d, color_mul(u, ahead), acc)
            behind = each(color_adj(u, project(1, d, x)), lambda v: shift(v, d, -1))
            acc = rebuild(1, d, behind, acc)
        return acc

    def z_hops(ahead, behind, o, acc):
        acc = rebuild(-1, 2, color_mul(link(o, 2), project(-1, 2, ahead)), acc)
        return rebuild(1, 2, color_adj(link(o - 1, 2), project(1, 2, behind)), acc)

    def t_hops(x, o, hbuf, gbuf, index, acc):
        u = link(o, 3)

        def joined(half, halo, by, at):
            return [
                tuple(
                    jnp.where(row == at, jnp.broadcast_to(q, (3, TP, 128)), pltpu.roll(v, by % TP, 1))
                    for v, q in zip(hv, qv)
                )
                for hv, qv in zip(half, halo)
            ]

        ahead = joined(project(-1, 3, x), get_halo(hbuf, index, top_flip), -1, T - 1)
        acc = rebuild(-1, 3, color_mul(u, ahead), acc)
        behind = joined(
            color_adj(u, project(1, 3, x)), get_halo(gbuf, index, bottom_flip), 1, 0
        )
        return rebuild(1, 3, behind, acc)

    zero = [(jnp.zeros((3, TP, 128), jnp.float32),) * 2] * 4

    def keep(s, acc):
        for sp in range(4):
            for p in range(2):
                acc_ref[s, pl.ds(p * 12 + sp * 3, 3)] = acc[sp][p]

    def kept(s):
        return [
            tuple(acc_ref[s, pl.ds(p * 12 + sp * 3, 3)] for p in range(2)) for sp in range(4)
        ]

    def updated(x, acc, i, s, write):
        rate = slots[s * NT, pl.ds(rows, 1), :]
        for sp in range(4):
            for p in range(2):
                for c in range(3):
                    comp = p * 12 + sp * 3 + c
                    b = sr[i, pl.ds((s * 24 + comp) * T, TP), :]
                    v = x[sp][p][c]
                    write(comp, v + rate * (b - (v - HOPPING * acc[sp][p][c])))

    def slot(offsets, o, s):
        return offsets.index(o % n) * S + s

    def loop(body):
        def step_body(s, carry):
            body(s)
            return carry

        lax.fori_loop(0, S, step_body, 0)

    loop(lambda s: keep(s, plane_hops(tile(xe0, s), 0, zero)))
    for copy in h_copies + g_copies:
        copy.wait_recv()
    loop(lambda s: keep(s, t_hops(tile(xe0, s), 0, hr0, gr0, s, kept(s))))
    for copy in xe_copies:
        copy.wait_recv()
    def first(i, o, s):
        x = tile(xe0, slot(d0, o, s))
        acc = kept(s) if i == 0 else plane_hops(x, o, zero)
        if i:
            acc = t_hops(x, o, hr0, gr0, i * S + s, acc)
        acc = z_hops(tile(xe0, slot(d0, o + 1, s)), tile(xe0, slot(d0, o - 1, s)), o, acc)

        def write(comp, v):
            xe1[i * S + s, pl.ds(comp, TP, stride=24), :] = v

        updated(x, acc, i, s, write)

    loop(lambda s: first(0, 0, s))

    edges_all(xe1, 1)
    h_next = send_halo(hs.at[1], hr1, h1_sem.at[0], h1_sem.at[1], below, [0])
    g_next = send_halo(gs.at[1], gr1, g1_sem.at[0], g1_sem.at[1], above, [0])
    for i in src_copies:
        src_copies[i].wait_recv()
    for i, o in enumerate(d1):
        if o:
            loop(lambda s: first(i, o, s))

    def inner(s):
        x = tile(xe1, s)
        acc = plane_hops(x, 0, zero)
        keep(s, z_hops(tile(xe1, slot(d1, 1, s)), tile(xe1, slot(d1, -1, s)), 0, acc))

    loop(inner)
    for copy in h_next + g_next:
        copy.wait_recv()

    def last(s):
        x = tile(xe1, s)
        acc = t_hops(x, 0, hr1, gr1, s, kept(s))

        def write(comp, v):
            sol[pl.ds((s * 24 + comp) * T, T), :] = v[0:T]

        updated(x, acc, 0, s, write)

    loop(last)
    for copy in sent + xe_copies + h_copies + g_copies + h_next + g_next:
        copy.wait_send()
    pltpu.make_async_copy(every, every, ar_send).wait()


def solution(mesh):
    n, L, U = mesh.shape["src"], mesh.shape["lat"], mesh.shape["sub"]

    def shards(sources, eigvecs, eigvals, links, damping):
        S, _, T, _, _ = sources.shape
        K, LZ = eigvecs.shape[0], links.shape[3]
        TP = -(-T // 8) * 8
        V = T * 24
        N = n * L * U
        rows = 2 * S * K // 128
        d0 = len(distinct((0, 1, -1, 2, -2), n))
        d1 = len(distinct((0, 1, -1), n))
        dl = len(distinct((0, 1, -1, -2), n))
        vmem = pl.BlockSpec(memory_space=pltpu.VMEM)
        smem = pl.BlockSpec(memory_space=pltpu.SMEM)
        f32 = jnp.float32
        dma = pltpu.SemaphoreType.DMA
        chunks = T // 2 if T % 2 == 0 else 1
        guess, result = pl.pallas_call(
            functools.partial(kernel, (T, LZ, S, K, TP), (n, L, U)),
            out_shape=[jax.ShapeDtypeStruct((S * V, 128), f32)] * 2,
            in_specs=[vmem, vmem, vmem, vmem, smem],
            out_specs=[vmem, vmem],
            scratch_shapes=[
                pltpu.VMEM((S, V, 128), f32),
                pltpu.VMEM((S, V, 128), f32),
                pltpu.VMEM((2 * S * K, 128), f32),
                pltpu.VMEM((N, rows + 1, 128), f32),
                pltpu.VMEM((2 * S * K, 128), f32),
                pltpu.VMEM((d0 * S, TP * 24, 128), f32),
                pltpu.VMEM((d1 * S, TP * 24, 128), f32),
                pltpu.VMEM((d1, S * V + 8, 128), f32),
                pltpu.VMEM((dl, 72, TP, 128), f32),
                pltpu.VMEM((2, S, 12, 1, 128), f32),
                pltpu.VMEM((2, S, 12, 1, 128), f32),
                pltpu.VMEM((d1 * S, 12, 1, 128), f32),
                pltpu.VMEM((d1 * S, 12, 1, 128), f32),
                pltpu.VMEM((S, 12, 1, 128), f32),
                pltpu.VMEM((S, 12, 1, 128), f32),
                pltpu.VMEM((S, 24, TP, 128), f32),
                dma, dma, dma((d1,)), dma((d1,)), dma((d0, chunks)), dma((d0, chunks)),
                dma((d1,)), dma((d1,)), dma((d1,)), dma((d1,)), dma((2, 1)), dma((2, 1)),
            ],
            compiler_params=pltpu.CompilerParams(
                collective_id=0, has_side_effects=True, vmem_limit_bytes=40 * 1024 * 1024
            ),
        )(
            sources.reshape(S * V, 128),
            eigvecs.transpose(0, 2, 3, 1, 4).reshape(K, V, 128),
            eigvals.reshape(1, K),
            links.reshape(72 * T * LZ, 128),
            damping,
        )
        return guess.reshape(sources.shape), result.reshape(sources.shape)

    spread = P(None, None, ("lat", "sub"), "src", None)
    return jax.shard_map(
        shards,
        mesh=mesh,
        in_specs=(spread, spread, P(), P(None, None, ("lat", "sub"), None, None), P("src")),
        out_specs=(spread, spread),
        check_vma=False,
    )
```

time: 96.9 us -> 31.8 us (0.33)
  blocking collectives: 42 us -> 0 us
  Pallas kernels: 0 us -> 25.1 us
  starting transfers between devices: 15.6 us -> 0 us
  other arithmetic: 14.4 us -> 0 us
  waiting for transfers between devices: 9.44 us -> 0 us
  local copies, waits for them, and re-layouts: 11.3 us -> 5.16 us
  between operations: 3.03 us -> 1.3 us
    psum x1 -> x0, blocking collectives: 42 us -> none  [shards(): correlation = lax.psum(partial_value, ('src', 'lat', 'sub'))]
    pallas_call x0 -> x1, Pallas kernels: none -> 25.1 us  [shards(): pl.pallas_call(functools.partial(kernel, (T, LZ, S, K, TP), (n, L, U)), o...]
    all_to_all x3 -> x0, starting transfers between devices: 10.9 us -> none  [the longest x1 3.89 us: shards(): lax.all_to_all(iterate, 'src', split_axis=3, concat_axis=0, tiled=True)]
    all_to_all x3 -> x0, waiting for transfers between devices: 6.94 us -> none  [the longest x1 4.67 us: shards(): lax.all_to_all(iterate, 'src', split_axis=3, concat_axis=0, tiled=True)]
    sub x71 -> x0, other arithmetic: 4.96 us -> none  [the longest x24 2.62 us: color_mul(): acc_re + links_re[row, col] * real_part[:, :, col]]
    slice x46 -> x0, local copies, waits for them, and re-layouts: 4.78 us -> none  [the longest x10 1.41 us: neighbour(): wrapped = jnp.roll(values, step * (LX - 1), axis=-1)]
    ppermute x4 -> x0, starting transfers between devices: 4.7 us -> none  [passed_along(): lax.ppermute(x, axis, [(i, (i + by) % devices) for i in range(devices)])]
    add x57 -> x0, other arithmetic: 4.55 us -> none  [the longest x20 2.11 us: color_adj(): acc_re + links_re[col, row] * real_part[:, :, col]]
  transfers between devices with their start and end apart: 7 -> 0, of which waited for: 3 -> 0; matrix products, arithmetic and copies ran while one was open for 13% -> 0% of each run, Pallas kernels for 0% -> 0%
where the time goes in v1:
time: 31.8 us; the launch traced here: 31.5 us
  Pallas kernels  25.1 us (79%)
  local copies, waits for them, and re-layouts  5.16 us (16%)
  between operations  1.3 us (4%)
    pallas_call x1, Pallas kernels, shards(): pl.pallas_call(functools.partial(kernel, (T, LZ, S, K, TP), (n, L, U)), o...  25.1 us
    unnamed x10, local copies, waits for them, and re-layouts  5.16 us

profile of v1, /device:TPU:0, one launch (start us, length us, event | category | flops | bytes accessed | tf_op | source)
XLA Modules:
  0.0 31.5 jit_solution(11347161096153198696)
XLA Ops:
  1.3 0.0 copy-start
  1.3 1.3 %copy-done = bf16[32,24,6,1,128]{4,1,3,2,0:T(8,128)(2,1)S(1)} copy-done((bf16[32,24,6,1,128]{4,1,3,2,0:T(8,128)(2,1)S(1)}, bf16[32,24,6,1,128]{4,1,3,2,0:T(8,128)(2,1)}, u32[]{:S(2)}) %copy-start) | copy-done | bytes 1179672
  2.5 0.0 copy-start.1
  2.6 1.0 %copy-done.1 = f32[4,18,6,2,128]{4,3,2,1,0:T(2,128)S(1)} copy-done((f32[4,18,6,2,128]{4,3,2,1,0:T(2,128)S(1)}, f32[4,18,6,2,128]{4,3,2,1,0:T(2,128)}, u32[]{:S(2)}) %copy-start.1) | copy-done | bytes 442392
  3.6 0.0 copy-start.2
  3.6 0.9 %copy-done.2 = f32[2,24,6,1,128]{4,3,2,1,0:T(1,128)S(1)} copy-done((f32[2,24,6,1,128]{4,3,2,1,0:T(1,128)S(1)}, f32[2,24,6,1,128]{4,3,2,1,0:T(1,128)}, u32[]{:S(2)}) %copy-start.2) | copy-done | bytes 147480
  4.5 0.0 copy-start.3
  4.5 0.7 %copy-done.3 = f32[32]{0:T(128)S(1)} copy-done((f32[32]{0:T(128)S(1)}, f32[32]{0:T(128)}, u32[]{:S(2)}) %copy-start.3) | copy-done | bytes 152
  5.1 25.1 %shard_map.68 = (f32[288,128]{1,0:T(8,128)S(1)}, f32[288,128]{1,0:T(8,128)S(1)}) custom-call(f32[288,128]{1,0:T(8,128)S(1)} %bitcast.10, bf16[32,144,128]{2,1,0:T(8,128)(2,1)S(1)} %bitcast.8, f32[1,32]{1,0:T(1,128)S(1)} %bitcast.13, f32[864,128]{1,0:T(8,128)S(1)} %bitcast.9, f32[1]{0:T(128)S(6)} %copy.13.damping), custom_call_target="tpu_custom_call" | custom-call | tf_op jit(solution)/shard_map/pallas_call | solution.py:435
  30.2 0.7 %copy.14 = f32[2,24,6,1,128]{4,3,2,1,0:T(1,128)} copy(f32[2,24,6,1,128]{4,3,2,1,0:T(1,128)S(1)} %bitcast.12) | data formatting | bytes 294912
  30.9 0.7 %copy.15 = f32[2,24,6,1,128]{4,3,2,1,0:T(1,128)} copy(f32[2,24,6,1,128]{4,3,2,1,0:T(1,128)S(1)} %bitcast.11) | data formatting | bytes 294912
Async XLA Ops:
  1.3 1.3 %copy-start = (bf16[32,24,6,1,128]{4,1,3,2,0:T(8,128)(2,1)S(1)}, bf16[32,24,6,1,128]{4,1,3,2,0:T(8,128)(2,1)}, u32[]{:S(2)}) copy-start(bf16[32,24,6,1,128]{4,1,3,2,0:T(8,128)(2,1)} %param.6) | copy-start | bytes 3538948
  2.5 1.0 %copy-start.1 = (f32[4,18,6,2,128]{4,3,2,1,0:T(2,128)S(1)}, f32[4,18,6,2,128]{4,3,2,1,0:T(2,128)}, u32[]{:S(2)}) copy-start(f32[4,18,6,2,128]{4,3,2,1,0:T(2,128)} %param.8) | copy-start | bytes 1327108
  3.6 0.9 %copy-start.2 = (f32[2,24,6,1,128]{4,3,2,1,0:T(1,128)S(1)}, f32[2,24,6,1,128]{4,3,2,1,0:T(1,128)}, u32[]{:S(2)}) copy-start(f32[2,24,6,1,128]{4,3,2,1,0:T(1,128)} %param.5) | copy-start | bytes 442372
  4.5 0.7 %copy-start.3 = (f32[32]{0:T(128)S(1)}, f32[32]{0:T(128)}, u32[]{:S(2)}) copy-start(f32[32]{0:T(128)} %param.7) | copy-start | bytes 388

commit v2 on v1

--- a/solution.py
+++ b/solution.py
@@ -9,6 +9,7 @@
 from jax.sharding import PartitionSpec as P
 
 LX = 16
+EIG_BLOCK = 8
 HOPPING = 0.12
 MESH = pl.DeviceIdType.MESH
 
@@ -83,7 +84,8 @@
 
 def kernel(
     shape, sizes,
-    src, eig, eigvals, links, damping, guess, sol,
+    src_hbm, eig_hbm, eigvals_hbm, links_hbm, damping_hbm, guess, sol,
+    src, eig, eigvals, links, damping, in_sem, eig_sem,
     sa, sb, corr, slots, w2, xe0, xe1, sr, le, hs, gs, hr0, gr0, hr1, gr1, acc_ref,
     ar_send, ar_recv, sr_send, sr_recv, xe_send, xe_recv, h_send, h_recv, g_send, g_recv,
     h1_sem, g1_sem,
@@ -117,7 +119,25 @@
         pl.semaphore_signal(barrier, inc=1, device_id=of(lax.rem(me + i, N)), device_id_type=MESH)
         return carry
 
+    parts = K // EIG_BLOCK
+    loads = [
+        pltpu.make_async_copy(a, b, in_sem.at[i])
+        for i, (a, b) in enumerate(
+            [(src_hbm, src), (damping_hbm, damping), (eigvals_hbm, eigvals), (links_hbm, links)]
+        )
+    ]
+    eig_loads = [
+        pltpu.make_async_copy(
+            eig_hbm.at[pl.ds(j * EIG_BLOCK, EIG_BLOCK)], eig.at[pl.ds(j * EIG_BLOCK, EIG_BLOCK)],
+            eig_sem.at[j],
+        )
+        for j in range(parts)
+    ]
+    loads[0].start()
     lax.fori_loop(1, N, greet, 0)
+    for copy in eig_loads + loads[1:]:
+        copy.start()
+    loads[0].wait()
 
     for s in range(S):
         for t in range(T):
@@ -140,17 +160,32 @@
                 corr[pl.ds((p * S + s) * K + k, 1), :] = jnp.sum(part, axis=0, keepdims=True)
         return carry
 
-    lax.fori_loop(0, K, correlate, 0)
+    sr[0, pl.ds(0, S * V), :] = src[...]
+    sent = []
+    src_copies = {}
+    for j in range(parts):
+        if j == parts // 2:
+            pl.semaphore_wait(barrier, N - 1)
+            for i, o in enumerate(d1):
+                if o:
+                    copy = pltpu.make_async_remote_copy(
+                        src_ref=src, dst_ref=sr.at[i, pl.ds(0, S * V)],
+                        send_sem=sr_send.at[i], recv_sem=sr_recv.at[i],
+                        device_id=device(lax.rem(me_s + n - o, n), place), device_id_type=MESH,
+                    )
+                    copy.start()
+                    sent.append(copy)
+                    src_copies[i] = copy
+        eig_loads[j].wait()
+        lax.fori_loop(j * EIG_BLOCK, (j + 1) * EIG_BLOCK, correlate, 0)
     flat = lax.dot_general(
         jnp.ones((8, 128), jnp.float32), corr[...], (((1,), (1,)), ((), ())),
         preferred_element_type=jnp.float32, precision=lax.Precision.HIGHEST,
     )
     for r in range(rows):
         slots[me, pl.ds(r, 1), :] = flat[0:1, r * 128 : (r + 1) * 128]
-    slots[me, pl.ds(rows, 1), :] = jnp.full((1, 128), damping[0], jnp.float32)
-    sr[0, pl.ds(0, S * V), :] = src[...]
-
-    pl.semaphore_wait(barrier, N - 1)
+    loads[1].wait()
+    slots[me, pl.ds(rows, 1), :] = jnp.broadcast_to(damping[...], (1, 128))
 
     def spread(i, carry):
         pltpu.make_async_remote_copy(
@@ -160,19 +195,8 @@
         return carry
 
     lax.fori_loop(1, N, spread, 0)
-
-    sent = []
-    src_copies = {}
-    for i, o in enumerate(d1):
-        if o:
-            copy = pltpu.make_async_remote_copy(
-                src_ref=src, dst_ref=sr.at[i, pl.ds(0, S * V)],
-                send_sem=sr_send.at[i], recv_sem=sr_recv.at[i],
-                device_id=device(lax.rem(me_s + n - o, n), place), device_id_type=MESH,
-            )
-            copy.start()
-            sent.append(copy)
-            src_copies[i] = copy
+    loads[2].wait()
+    loads[3].wait()
 
     for i, o in enumerate(dl):
         z = lax.rem(me_s + o, n)
@@ -428,16 +452,22 @@
         d1 = len(distinct((0, 1, -1), n))
         dl = len(distinct((0, 1, -1, -2), n))
         vmem = pl.BlockSpec(memory_space=pltpu.VMEM)
-        smem = pl.BlockSpec(memory_space=pltpu.SMEM)
+        hbm = pl.BlockSpec(memory_space=pltpu.HBM)
         f32 = jnp.float32
         dma = pltpu.SemaphoreType.DMA
         chunks = T // 2 if T % 2 == 0 else 1
         guess, result = pl.pallas_call(
             functools.partial(kernel, (T, LZ, S, K, TP), (n, L, U)),
             out_shape=[jax.ShapeDtypeStruct((S * V, 128), f32)] * 2,
-            in_specs=[vmem, vmem, vmem, vmem, smem],
+            in_specs=[hbm] * 5,
             out_specs=[vmem, vmem],
             scratch_shapes=[
+                pltpu.VMEM((S * V, 128), f32),
+                pltpu.VMEM((K, V, 128), jnp.bfloat16),
+                pltpu.VMEM((1, K), f32),
+                pltpu.VMEM((72 * T * LZ, 128), f32),
+                pltpu.VMEM((1, 1), f32),
+                dma((4,)), dma((K // EIG_BLOCK,)),
                 pltpu.VMEM((S, V, 128), f32),
                 pltpu.VMEM((S, V, 128), f32),
                 pltpu.VMEM((2 * S * K, 128), f32),
@@ -458,14 +488,14 @@
                 dma((d1,)), dma((d1,)), dma((d1,)), dma((d1,)), dma((2, 1)), dma((2, 1)),
             ],
             compiler_params=pltpu.CompilerParams(
-                collective_id=0, has_side_effects=True, vmem_limit_bytes=40 * 1024 * 1024
+                collective_id=0, has_side_effects=True, vmem_limit_bytes=63 * 1024 * 1024
             ),
         )(
             sources.reshape(S * V, 128),
             eigvecs.transpose(0, 2, 3, 1, 4).reshape(K, V, 128),
             eigvals.reshape(1, K),
             links.reshape(72 * T * LZ, 128),
-            damping,
+            damping.reshape(1, 1),
         )
         return guess.reshape(sources.shape), result.reshape(sources.shape)
 

time: 31.8 us -> 34 us (1.069)
  Pallas kernels: 25.1 us -> 29.3 us
  local copies, waits for them, and re-layouts: 5.16 us -> 3.21 us
    pallas_call x1, Pallas kernels: 25.1 us -> 29.3 us  [shards(): pl.pallas_call(functools.partial(kernel, (T, LZ, S, K, TP), (n, L, U)), o...]
    unnamed x10 -> x2, local copies, waits for them, and re-layouts: 5.16 us -> 3.21 us
where the time goes in v2:
time: 34 us; the launch traced here: 33.8 us
  Pallas kernels  29.3 us (86%)
  local copies, waits for them, and re-layouts  3.21 us (9%)
  between operations  1.29 us (4%)
    pallas_call x1, Pallas kernels, shards(): pl.pallas_call(functools.partial(kernel, (T, LZ, S, K, TP), (n, L, U)), o...  29.3 us
    unnamed x2, local copies, waits for them, and re-layouts  3.21 us

profile of v2, /device:TPU:0, one launch (start us, length us, event | category | flops | bytes accessed | tf_op | source)
XLA Modules:
  0.0 33.8 jit_solution(17771640797764178959)
XLA Ops:
  1.3 29.3 %shard_map.68 = (f32[288,128]{1,0:T(8,128)}, f32[288,128]{1,0:T(8,128)}) custom-call(f32[288,128]{1,0:T(8,128)} %bitcast.12, bf16[32,144,128]{2,1,0:T(8,128)(2,1)} %bitcast.10, f32[1,32]{1,0:T(1,128)} %bitcast.15, f32[864,128]{1,0:T(8,128)} %bitcast.11, f32[1,1]{1,0:T(1,128)} %bitcast.9.damping_hbm), custom_call_target="tpu_custom_call" | custom-call | tf_op jit(solution)/shard_map/pallas_call | solution.py:459
  30.6 1.6 %copy.14 = f32[2,24,6,1,128]{4,3,2,1,0:T(1,128)} copy(f32[2,24,6,1,128]{4,3,2,1,0:T(1,128)} %bitcast.14) | data formatting | bytes 294912
  32.2 1.6 %copy.15 = f32[2,24,6,1,128]{4,3,2,1,0:T(1,128)} copy(f32[2,24,6,1,128]{4,3,2,1,0:T(1,128)} %bitcast.13) | data formatting | bytes 294912

commit v3 on v2

--- a/solution.py
+++ b/solution.py
@@ -166,16 +166,6 @@
     for j in range(parts):
         if j == parts // 2:
             pl.semaphore_wait(barrier, N - 1)
-            for i, o in enumerate(d1):
-                if o:
-                    copy = pltpu.make_async_remote_copy(
-                        src_ref=src, dst_ref=sr.at[i, pl.ds(0, S * V)],
-                        send_sem=sr_send.at[i], recv_sem=sr_recv.at[i],
-                        device_id=device(lax.rem(me_s + n - o, n), place), device_id_type=MESH,
-                    )
-                    copy.start()
-                    sent.append(copy)
-                    src_copies[i] = copy
         eig_loads[j].wait()
         lax.fori_loop(j * EIG_BLOCK, (j + 1) * EIG_BLOCK, correlate, 0)
     flat = lax.dot_general(
@@ -195,6 +185,16 @@
         return carry
 
     lax.fori_loop(1, N, spread, 0)
+    for i, o in enumerate(d1):
+        if o:
+            copy = pltpu.make_async_remote_copy(
+                src_ref=src, dst_ref=sr.at[i, pl.ds(0, S * V)],
+                send_sem=sr_send.at[i], recv_sem=sr_recv.at[i],
+                device_id=device(lax.rem(me_s + n - o, n), place), device_id_type=MESH,
+            )
+            copy.start()
+            sent.append(copy)
+            src_copies[i] = copy
     loads[2].wait()
     loads[3].wait()
 
@@ -458,7 +458,7 @@
         chunks = T // 2 if T % 2 == 0 else 1
         guess, result = pl.pallas_call(
             functools.partial(kernel, (T, LZ, S, K, TP), (n, L, U)),
-            out_shape=[jax.ShapeDtypeStruct((S * V, 128), f32)] * 2,
+            out_shape=[pltpu.VMEM((S * V, 128), f32)] * 2,
             in_specs=[hbm] * 5,
             out_specs=[vmem, vmem],
             scratch_shapes=[
@@ -488,7 +488,7 @@
                 dma((d1,)), dma((d1,)), dma((d1,)), dma((d1,)), dma((2, 1)), dma((2, 1)),
             ],
             compiler_params=pltpu.CompilerParams(
-                collective_id=0, has_side_effects=True, vmem_limit_bytes=63 * 1024 * 1024
+                collective_id=0, has_side_effects=True, vmem_limit_bytes=61000 * 1024
             ),
         )(
             sources.reshape(S * V, 128),

time: 34 us -> 29.2 us (0.86)
  Pallas kernels: 29.3 us -> 26.5 us
  local copies, waits for them, and re-layouts: 3.21 us -> 1.32 us
    pallas_call x1, Pallas kernels: 29.3 us -> 26.5 us  [shards(): pl.pallas_call(functools.partial(kernel, (T, LZ, S, K, TP), (n, L, U)), o...]
    unnamed x2, local copies, waits for them, and re-layouts: 3.21 us -> 1.32 us
where the time goes in v3:
time: 29.2 us; the launch traced here: 29.1 us
  Pallas kernels  26.5 us (91%)
  local copies, waits for them, and re-layouts  1.32 us (5%)
  between operations  1.29 us (4%)
    pallas_call x1, Pallas kernels, shards(): pl.pallas_call(functools.partial(kernel, (T, LZ, S, K, TP), (n, L, U)), o...  26.5 us
    unnamed x2, local copies, waits for them, and re-layouts  1.32 us

profile of v3, /device:TPU:0, one launch (start us, length us, event | category | flops | bytes accessed | tf_op | source)
XLA Modules:
  0.0 29.1 jit_solution(10049868115177563418)
XLA Ops:
  1.3 26.5 %shard_map.68 = (f32[288,128]{1,0:T(8,128)S(1)}, f32[288,128]{1,0:T(8,128)S(1)}) custom-call(f32[288,128]{1,0:T(8,128)} %bitcast.14, bf16[32,144,128]{2,1,0:T(8,128)(2,1)} %bitcast.12, f32[1,32]{1,0:T(1,128)} %bitcast.15, f32[864,128]{1,0:T(8,128)} %bitcast.13, f32[1,1]{1,0:T(1,128)} %bitcast.9.damping_hbm), custom_call_target="tpu_custom_call" | custom-call | tf_op jit(solution)/shard_map/pallas_call | solution.py:459
  27.7 0.7 %copy.13 = f32[2,24,6,1,128]{4,3,2,1,0:T(1,128)} copy(f32[2,24,6,1,128]{4,3,2,1,0:T(1,128)S(1)} %bitcast.11) | data formatting | bytes 294912
  28.4 0.7 %copy.14 = f32[2,24,6,1,128]{4,3,2,1,0:T(1,128)} copy(f32[2,24,6,1,128]{4,3,2,1,0:T(1,128)S(1)} %bitcast.10) | data formatting | bytes 294912

commit v4 on v3

--- a/solution.py
+++ b/solution.py
@@ -167,7 +167,7 @@
         if j == parts // 2:
             pl.semaphore_wait(barrier, N - 1)
         eig_loads[j].wait()
-        lax.fori_loop(j * EIG_BLOCK, (j + 1) * EIG_BLOCK, correlate, 0)
+        lax.fori_loop(j * EIG_BLOCK, (j + 1) * EIG_BLOCK, correlate, 0, unroll=4)
     flat = lax.dot_general(
         jnp.ones((8, 128), jnp.float32), corr[...], (((1,), (1,)), ((), ())),
         preferred_element_type=jnp.float32, precision=lax.Precision.HIGHEST,
@@ -284,7 +284,7 @@
             )
 
         acc = lax.fori_loop(
-            0, K, mix, tuple(jnp.zeros((step, 128), jnp.float32) for _ in range(2 * S)), unroll=4
+            0, K, mix, tuple(jnp.zeros((step, 128), jnp.float32) for _ in range(2 * S)), unroll=8
         )
         for s in range(S):
             one, two = acc[s], acc[S + s]

time: 29.2 us -> 29.1 us (level)
  no operation moved by 1% of the time
where the time goes in v4:
time: 29.1 us; the launch traced here: 28.9 us
  Pallas kernels  26.3 us (90%)
  local copies, waits for them, and re-layouts  1.32 us (5%)
  between operations  1.29 us (4%)
    pallas_call x1, Pallas kernels, shards(): pl.pallas_call(functools.partial(kernel, (T, LZ, S, K, TP), (n, L, U)), o...  26.3 us
    unnamed x2, local copies, waits for them, and re-layouts  1.32 us

profile of v4, /device:TPU:0, one launch (start us, length us, event | category | flops | bytes accessed | tf_op | source)
XLA Modules:
  0.0 28.9 jit_solution(3952249613903716337)
XLA Ops:
  1.3 26.3 %shard_map.68 = (f32[288,128]{1,0:T(8,128)S(1)}, f32[288,128]{1,0:T(8,128)S(1)}) custom-call(f32[288,128]{1,0:T(8,128)} %bitcast.14, bf16[32,144,128]{2,1,0:T(8,128)(2,1)} %bitcast.12, f32[1,32]{1,0:T(1,128)} %bitcast.15, f32[864,128]{1,0:T(8,128)} %bitcast.13, f32[1,1]{1,0:T(1,128)} %bitcast.9.damping_hbm), custom_call_target="tpu_custom_call" | custom-call | tf_op jit(solution)/shard_map/pallas_call | solution.py:459
  27.6 0.7 %copy.13 = f32[2,24,6,1,128]{4,3,2,1,0:T(1,128)} copy(f32[2,24,6,1,128]{4,3,2,1,0:T(1,128)S(1)} %bitcast.11) | data formatting | bytes 294912
  28.3 0.7 %copy.14 = f32[2,24,6,1,128]{4,3,2,1,0:T(1,128)} copy(f32[2,24,6,1,128]{4,3,2,1,0:T(1,128)S(1)} %bitcast.10) | data formatting | bytes 294912
